TPU v7x, 32 devices: a whole 2x2x4 slice. The times are simulated.
32 devices in a mesh: mode: 4 (over y, x), mesh: 8 (over z, core).
Axes of the slice: x: 2, y: 2, z: 4, core: 2. Of those that a mesh axis runs over, the one named last changes fastest.
Arguments:
- b_field: float32 [128, 2, 3, 16384], P('mode', None, None, 'mesh'), may hold values from -6 to 6
- nu_coef: float32 [2, 17, 16384], P(None, None, 'mesh'), may hold values from -4 to 4
- nu_modes: int32 [17], replicated, may hold values from 0 to 127, as said below
- inv_mass: float32 [16384], P('mesh'), may hold values from 0.5 to 2
- connect: int32 [6, 8192], P(None, 'mesh'), may hold values from 0 to 2047
- stiff_plane: float32 [6, 6, 8192], P(None, None, 'mesh'), as said below
- stiff_mode: float32 [6, 6, 8192], P(None, None, 'mesh'), as said below
- shared_nodes: int32 [8, 2, 128], P('mesh'), may hold values from 0 to 2047, as said below
Outputs:
- b_next: float32 [128, 2, 3, 16384], P('mode', None, None, 'mesh')
Inputs may be any that keep to these rules, and one draw needn't show every extreme that they name: `nu_modes`: the 17 mode numbers are distinct. `shared_nodes`: in each partition the 256 entries are distinct local nodes. `stiff_plane`: each element matrix is symmetric. `stiff_mode`: each element matrix is symmetric.
All inputs are finite; a program needn't handle non-finite values.
Results may differ from a plain program's by a relative error of at most 0.000075.
Values sent between devices are 32-bit elements; how exact they have to be, the bound alone decides.
A program may use at most 128 MiB of HBM per device.

v0:
```python
import functools
import jax
import jax.numpy as jnp
from jax import lax
from jax.experimental import pallas as pl
from jax.experimental.pallas import tpu as pltpu
from jax.sharding import PartitionSpec as P

time_step = 0.1
f32, bf16 = jnp.float32, jnp.bfloat16
lanes = 128
tile = 256


def from_behind(block, axis, distance):
    devices = range(lax.axis_size(axis))
    route = [(i - distance, i) for i in devices if i - distance in devices]
    return lax.ppermute(block, axis, route)


def halves(value):
    high = value.astype(bf16)
    return high, (value - high.astype(f32)).astype(bf16)


def lane_slice(index, width):
    return pl.ds(pl.multiple_of(index * width, width), width)


def fill_select(shared_ref, select_ref):
    nloc = select_ref.shape[0]
    ids = lax.broadcasted_iota(jnp.int32, (nloc, lanes), 0)
    for side in range(2):
        hit = ids == shared_ref[side : side + 1, :]
        select_ref[:, side * lanes : (side + 1) * lanes] = jnp.where(hit, 1.0, 0.0).astype(bf16)


def received_at(got_ref, split_ref, select_ref, cols):
    rows = got_ref.shape[1]
    both = lax.dot_general(
        split_ref[...], select_ref[cols, :], (((1,), (1,)), ((), ())), preferred_element_type=f32
    )
    return both[:rows] + both[rows:]


def split_received(got_ref, split_ref):
    rows = got_ref.shape[1]
    for side in range(2):
        high, low = halves(got_ref[side])
        split_ref[:rows, side * lanes : (side + 1) * lanes] = high
        split_ref[rows:, side * lanes : (side + 1) * lanes] = low


def couple(x_ref, coef_ref, nu_modes_ref, h_ref):
    pieces, total = x_ref.shape[1], x_ref.shape[2] // 2
    rows = 2 * total
    step = 64

    @pl.loop(0, pieces)
    def _(nt):
        cols = lane_slice(nt, lanes)
        for start in range(0, total, step):
            re = jnp.zeros((step, lanes), f32)
            im = jnp.zeros((step, lanes), f32)
            for j in range(coef_ref.shape[1]):
                begin = total + start - nu_modes_ref[j]
                xr = x_ref[0, nt, pl.ds(begin, step), :]
                xi = x_ref[1, nt, pl.ds(begin, step), :]
                cr = coef_ref[0, j : j + 1, cols]
                ci = coef_ref[1, j : j + 1, cols]
                re = re + (cr * xr - ci * xi)
                im = im + (cr * xi + ci * xr)
            for part, value in ((0, re), (1, im)):
                high, low = halves(value)
                base = part * total + start
                h_ref[base : base + step, cols] = high
                h_ref[rows + base : rows + base + step, cols] = low


def stiffness(h_ref, connect_ref, plane_ref, mode_ref, t_ref, p_ref, y_ref, z_ref):
    rows, nloc = z_ref.shape
    total = rows // 2
    elems = connect_ref.shape[1]
    z_ref[...] = jnp.zeros_like(z_ref)
    chunk = 256
    band = 16

    @pl.loop(0, elems // tile)
    def _(t):
        @pl.loop(0, nloc // chunk)
        def _(n):
            ids = lax.broadcasted_iota(jnp.int32, (chunk, tile), 0) + n * chunk
            for a in range(6):
                hit = ids == connect_ref[a : a + 1, lane_slice(t, tile)]
                t_ref[lane_slice(n, chunk), a * tile : (a + 1) * tile] = jnp.where(
                    hit, 1.0, 0.0
                ).astype(bf16)

        @pl.loop(0, 6)
        def _(a):
            both = jnp.dot(h_ref[...], t_ref[:, lane_slice(a, tile)], preferred_element_type=f32)
            p_ref[a] = both[:rows] + both[rows:]

        @pl.loop(0, total // band)
        def _(g):
            at = pl.multiple_of(g * band, band)
            m = lax.broadcasted_iota(jnp.int32, (band, lanes), 0) + at
            mm = jnp.minimum(m, total - m).astype(f32)
            weight = mm * mm
            for piece in range(tile // lanes):
                cols = pl.ds(pl.multiple_of(t * tile + piece * lanes, lanes), lanes)
                near = slice(piece * lanes, (piece + 1) * lanes)
                picked = [
                    [p_ref[a, pl.ds(part * total + at, band), near] for a in range(6)]
                    for part in range(2)
                ]
                y = [[jnp.zeros((band, lanes), f32)] * 6 for part in range(2)]
                for b in range(6):
                    for a in range(b, 6):
                        s = plane_ref[b, a : a + 1, cols] + weight * mode_ref[b, a : a + 1, cols]
                        for part in range(2):
                            y[part][b] = y[part][b] + s * picked[part][a]
                            if a != b:
                                y[part][a] = y[part][a] + s * picked[part][b]
                for part in range(2):
                    for b in range(6):
                        high, low = halves(y[part][b])
                        here = slice(b * tile + piece * lanes, b * tile + (piece + 1) * lanes)
                        base = part * total + at
                        y_ref[pl.ds(pl.multiple_of(base, band), band), here] = high
                        y_ref[pl.ds(pl.multiple_of(rows + base, band), band), here] = low

        @pl.loop(0, nloc // chunk)
        def _(n):
            cols = lane_slice(n, chunk)
            both = lax.dot_general(
                y_ref[...],
                t_ref[cols, :],
                (((1,), (1,)), ((), ())),
                preferred_element_type=f32,
            )
            z_ref[:, cols] += both[:rows] + both[rows:]


def send_values(z_ref, h_ref, select_ref, sent_ref):
    rows = z_ref.shape[0]

    @pl.loop(0, z_ref.shape[1] // 256)
    def _(n):
        cols = lane_slice(n, 256)
        high, low = halves(z_ref[:, cols])
        h_ref[:rows, cols] = high
        h_ref[rows:, cols] = low

    both = jnp.dot(h_ref[...], select_ref[...], preferred_element_type=f32)
    both = both[:rows] + both[rows:]
    sent_ref[0] = both[:, :lanes]
    sent_ref[1] = both[:, lanes:]


def put_field(x_ref, part, nt, start, value):
    total = x_ref.shape[2] // 2
    count = value.shape[0]
    x_ref[part, nt, start : start + count, :] = value
    x_ref[part, nt, total + start : total + start + count, :] = value


def first_kernel(
    nu_modes_ref, b_ref, coef_ref, connect_ref, plane_ref, mode_ref, shared_ref,
    z_ref, sent_ref, x_ref, h_ref, t_ref, p_ref, y_ref, select_ref,
):
    sources, _, count, nloc = b_ref.shape
    fill_select(shared_ref, select_ref)

    @pl.loop(0, nloc // lanes)
    def _(nt):
        for source in range(sources):
            for part in range(2):
                put_field(x_ref, part, nt, source * count, b_ref[source, part, :, lane_slice(nt, lanes)])

    couple(x_ref, coef_ref, nu_modes_ref, h_ref)
    stiffness(h_ref, connect_ref, plane_ref, mode_ref, t_ref, p_ref, y_ref, z_ref)
    send_values(z_ref, h_ref, select_ref, sent_ref)


def second_kernel(
    nu_modes_ref, b_ref, coef_ref, connect_ref, plane_ref, mode_ref, shared_ref,
    inv_ref, z1_ref, got_ref,
    z_ref, sent_ref, mid_ref, x_ref, h_ref, t_ref, p_ref, y_ref, select_ref, split_ref,
):
    sources, _, count, nloc = b_ref.shape
    total = sources * count
    fill_select(shared_ref, select_ref)
    split_received(got_ref, split_ref)

    @pl.loop(0, nloc // tile)
    def _(n):
        added = received_at(got_ref, split_ref, select_ref, lane_slice(n, tile))
        for piece in range(tile // lanes):
            nt = n * (tile // lanes) + piece
            cols = lane_slice(nt, lanes)
            drop = -time_step * inv_ref[:, cols]
            for source in range(sources):
                for part in range(2):
                    base = part * total + source * count
                    s = z1_ref[base : base + count, cols]
                    s = s + added[base : base + count, piece * lanes : (piece + 1) * lanes]
                    value = b_ref[source, part, :, cols] + drop * s
                    mid_ref[source, part, :, cols] = value
                    put_field(x_ref, part, nt, source * count, value)

    couple(x_ref, coef_ref, nu_modes_ref, h_ref)
    stiffness(h_ref, connect_ref, plane_ref, mode_ref, t_ref, p_ref, y_ref, z_ref)
    send_values(z_ref, h_ref, select_ref, sent_ref)


def last_kernel(
    b_ref, mid_ref, shared_ref, inv_ref, z_ref, got_ref, out_ref, select_ref, split_ref
):
    sources, _, count, nloc = b_ref.shape
    total = sources * count
    fill_select(shared_ref, select_ref)
    split_received(got_ref, split_ref)

    @pl.loop(0, nloc // tile)
    def _(n):
        cols = lane_slice(n, tile)
        added = received_at(got_ref, split_ref, select_ref, cols)
        drop = -time_step * inv_ref[:, cols]
        for source in range(sources):
            for part in range(2):
                base = part * total + source * count
                s = z_ref[base : base + count, cols] + added[base : base + count]
                value = mid_ref[source, part, :, cols] + drop * s
                out_ref[source, part, :, cols] = 0.5 * b_ref[source, part, :, cols] + 0.5 * value


def exchange(sent):
    below = from_behind(sent[1], "mesh", 1)
    above = from_behind(sent[0], "mesh", -1)
    return jnp.stack([below, above])


def body(b_field, nu_coef, nu_modes, inv_mass, connect, stiff_plane, stiff_mode, shared_nodes):
    count, _, comps, nloc = b_field.shape
    sources = lax.axis_size("mode")
    total = sources * count
    rows = 2 * total
    parts = jnp.transpose(b_field, (2, 1, 0, 3))
    parts = jnp.pad(parts, ((0, sources - comps), (0, 0), (0, 0), (0, 0)))
    mine = lax.all_to_all(parts, "mode", 0, 0, tiled=True)
    inv = inv_mass[None, :]
    shared = shared_nodes[0]
    vmem = pl.BlockSpec(memory_space=pltpu.VMEM)
    smem = pl.BlockSpec(memory_space=pltpu.SMEM)
    params = pltpu.CompilerParams(vmem_limit_bytes=56 * 1024 * 1024)
    scratch = [
        pltpu.VMEM((2, nloc // lanes, 2 * total, lanes), f32),
        pltpu.VMEM((2 * rows, nloc), bf16),
        pltpu.VMEM((nloc, 6 * tile), bf16),
        pltpu.VMEM((6, rows, tile), f32),
        pltpu.VMEM((2 * rows, 6 * tile), bf16),
        pltpu.VMEM((nloc, 2 * lanes), bf16),
    ]
    split = pltpu.VMEM((2 * rows, 2 * lanes), bf16)
    z_shape = jax.ShapeDtypeStruct((rows, nloc), f32)
    sent_shape = jax.ShapeDtypeStruct((2, rows, lanes), f32)
    field_shape = jax.ShapeDtypeStruct(mine.shape, f32)
    fixed = (nu_coef, connect, stiff_plane, stiff_mode, shared)
    z1, sent = pl.pallas_call(
        first_kernel, out_shape=(z_shape, sent_shape), in_specs=[smem] + [vmem] * 6,
        out_specs=(vmem, vmem), scratch_shapes=scratch, compiler_params=params,
    )(nu_modes, mine, *fixed)
    z2, sent2, mid = pl.pallas_call(
        second_kernel, out_shape=(z_shape, sent_shape, field_shape), in_specs=[smem] + [vmem] * 9,
        out_specs=(vmem, vmem, vmem), scratch_shapes=scratch + [split], compiler_params=params,
    )(nu_modes, mine, *fixed, inv, z1, exchange(sent))
    done = pl.pallas_call(
        last_kernel, out_shape=field_shape, in_specs=[vmem] * 6, out_specs=vmem,
        scratch_shapes=[scratch[-1], split], compiler_params=params,
    )(mine, mid, shared, inv, z2, exchange(sent2))
    back = lax.all_to_all(done, "mode", 0, 0, tiled=True)
    return jnp.transpose(back[:comps], (2, 1, 0, 3))


def solution(mesh):
    placed = (
        P("mode", None, None, "mesh"),
        P(None, None, "mesh"),
        P(),
        P("mesh"),
        P(None, "mesh"),
        P(None, None, "mesh"),
        P(None, None, "mesh"),
        P("mesh", None, None),
    )
    return jax.shard_map(
        body, mesh=mesh, in_specs=placed, out_specs=P("mode", None, None, "mesh"), check_vma=False
    )
```

profile of v0, /device:TPU:9, one launch (start us, length us, event | category | flops | bytes accessed | tf_op | source)
XLA Modules:
  0.0 214.5 jit_solution(17893172249066684480)
XLA Ops:
  0.0 2.3 %copy.14 = f32[32,2,3,2048]{3,0,1,2:T(8,128)S(1)} copy(f32[32,2,3,2048]{3,1,2,0:T(2,128)} %param.8) | data formatting | bytes 3145728 | tf_op args[0]
  2.3 1.6 pad.4
  3.9 0.0 copy-start.1
  3.9 3.7 %all-to-all-start = ((f32[4,2,32,2048]{3,2,1,0:T(8,128)}), f32[4,2,32,2048]{3,2,1,0:T(8,128)S(1)}, u32[]{:S(2)}, u32[]{:S(2)}) async-start(f32[4,2,32,2048]{3,2,1,0:T(8,128)} %pad.4), calls=%async_computation | async-start | bytes 4194304 | tf_op jit(solution)/shard_map/all_to_all | solution.py:251
  7.6 0.0 copy-done.1
  7.6 0.9 copy.11.coef_ref
  8.6 23.4 %all-to-all-done.b_ref = f32[4,2,32,2048]{3,2,1,0:T(8,128)S(1)} async-done(((f32[4,2,32,2048]{3,2,1,0:T(8,128)}), f32[4,2,32,2048]{3,2,1,0:T(8,128)S(1)}, u32[]{:S(2)}, u32[]{:S(2)}) %all-to-all-start) | async-done | bytes 2097184 | tf_op jit(solution)/shard_map/all_to_all | solution.py:251
  31.9 0.0 copy-start
  31.9 1.3 copy-done
  33.3 58.9 %shard_map.82 = (f32[256,2048]{1,0:T(8,128)}, f32[2,256,128]{2,1,0:T(8,128)}) custom-call(s32[17]{0:T(128)} %nu_modes_ref.3, f32[4,2,32,2048]{3,2,1,0:T(8,128)} %copy-done, f32[2,17,2048]{2,1,0:T(8,128)} %copy.11.coef_ref, s32[6,1024]{1,0:T(8,128)} %connect_ref.3, f32[6,6,1024]{2,1,0:T(8,128)} %plane_ref.3, f32[6,6,1024]{2,1,0:T(8,128)} %mode_ref.3, ...), custom_call_target="tpu_custom_call" | custom-call | tf_op jit(solution)/shard_map/pallas_call | solution.py:270
  92.2 1.0 slice_bitcast_fusion.4
  93.1 4.5 %collective-permute-start = (f32[256,128]{1,0:T(8,128)S(1)}, f32[256,128]{1,0:T(8,128)S(1)}, u32[]{:S(2)}, u32[]{:S(2)}) collective-permute-start(f32[256,128]{1,0:T(8,128)S(1)} %get-tuple-element.17), channel_id=1, source_target_pairs={{0,1},{1,2},{2,3},{3,4},{4,5},{5,6},{6,7},{8,9},{9,10},{10,11},{11... | collective-permute-start | bytes 393224 | tf_op jit(solution)/shard_map/ppermute | solution.py:18
  97.7 1.9 collective-permute-start.1
  99.6 0.0 collective-permute-done
  99.6 4.3 %collective-permute-done.1 = f32[256,128]{1,0:T(8,128)S(1)} collective-permute-done((f32[256,128]{1,0:T(8,128)S(1)}, f32[256,128]{1,0:T(8,128)S(1)}, u32[]{:S(2)}, u32[]{:S(2)}) %collective-permute-start.1) | collective-permute-done | bytes 131104 | tf_op jit(solution)/shard_map/ppermute | solution.py:18
  104.0 0.7 pad_maximum_fusion.got_ref
  104.7 62.3 %shard_map.83 = (f32[256,2048]{1,0:T(8,128)}, f32[2,256,128]{2,1,0:T(8,128)}, f32[4,2,32,2048]{3,2,1,0:T(8,128)}) custom-call(s32[17]{0:T(128)} %nu_modes_ref.3, f32[4,2,32,2048]{3,2,1,0:T(8,128)} %copy-done, f32[2,17,2048]{2,1,0:T(8,128)} %copy.11.coef_ref, s32[6,1024]{1,0:T(8,128)} %connect_ref.3, f32[6,6,1024]{2,1,0:T(8,128)} %plane_ref.3, ...), custom_call_target="tpu_custom_call" | custom-call | tf_op jit(solution)/shard_map/pallas_call | solution.py:274
  167.0 1.0 slice_bitcast_fusion.2
  168.0 1.9 collective-permute-start.2
  169.9 2.4 %collective-permute-start.3 = (f32[256,128]{1,0:T(8,128)S(1)}, f32[256,128]{1,0:T(8,128)S(1)}, u32[]{:S(2)}, u32[]{:S(2)}) collective-permute-start(f32[256,128]{1,0:T(8,128)S(1)} %get-tuple-element.16), channel_id=1, source_target_pairs={{1,0},{2,1},{3,2},{4,3},{5,4},{6,5},{7,6},{9,8},{10,9},{11,10},{12... | collective-permute-start | bytes 393224 | tf_op jit(solution)/shard_map/ppermute | solution.py:18
  172.3 0.0 collective-permute-done.2
  172.4 3.9 %collective-permute-done.3 = f32[256,128]{1,0:T(8,128)S(1)} collective-permute-done((f32[256,128]{1,0:T(8,128)S(1)}, f32[256,128]{1,0:T(8,128)S(1)}, u32[]{:S(2)}, u32[]{:S(2)}) %collective-permute-start.3) | collective-permute-done | bytes 131104 | tf_op jit(solution)/shard_map/ppermute | solution.py:18
  176.2 0.7 pad_maximum_fusion.1.got_ref
  176.9 6.7 %shard_map.84 = f32[4,2,32,2048]{3,2,1,0:T(8,128)} custom-call(f32[4,2,32,2048]{3,2,1,0:T(8,128)} %copy-done, f32[4,2,32,2048]{3,2,1,0:T(8,128)} %get-tuple-element.12.mid_ref, s32[2,128]{1,0:T(2,128)} %bitcast.28, f32[1,2048]{1,0:T(1,128)} %bitcast.25, f32[256,2048]{1,0:T(8,128)} %get-tuple-element.13.z_ref, f32[2,256,128]{2,1,0:T(8,128)} %pad_maximum_fusion.1.got_ref), custom_call_target="tpu_custom_call" | custom-call | tf_op jit(solution)/shard_map/pallas_call | solution.py:278
  183.7 28.4 %all_to_all.10 = f32[4,2,32,2048]{3,2,1,0:T(8,128)S(1)} all-to-all(f32[4,2,32,2048]{3,2,1,0:T(8,128)} %shard_map.84), channel_id=1, replica_groups=mesh['mode'=4,'mesh'=8] {'mode'}, dimensions={0} | all-to-all | bytes 4194304 | tf_op jit(solution)/shard_map/all_to_all | solution.py:282
  212.1 0.1 slice_bitcast_fusion
  212.2 2.4 %copy.12 = f32[32,2,3,2048]{3,1,2,0:T(2,128)} copy(f32[32,2,3,2048]{3,0,1,2:T(8,128)S(1)} %slice_bitcast_fusion) | data formatting | bytes 3145728 | tf_op jit(solution)/shard_map/transpose | solution.py:283
Async XLA Ops:
  3.9 3.8 %copy-start.1 = (f32[2,17,2048]{2,0,1:T(2,128)S(1)}, f32[2,17,2048]{2,0,1:T(2,128)}, u32[]{:S(2)}) copy-start(f32[2,17,2048]{2,0,1:T(2,128)} %param.9) | copy-start | bytes 835588
  3.9 28.1 %all-to-all-start = ((f32[4,2,32,2048]{3,2,1,0:T(8,128)}), f32[4,2,32,2048]{3,2,1,0:T(8,128)S(1)}, u32[]{:S(2)}, u32[]{:S(2)}) async-start(f32[4,2,32,2048]{3,2,1,0:T(8,128)} %pad.4), calls=%async_computation | async-start | bytes 4194304 | tf_op jit(solution)/shard_map/all_to_all | solution.py:251
  31.9 1.3 copy-start
  93.1 6.5 %collective-permute-start = (f32[256,128]{1,0:T(8,128)S(1)}, f32[256,128]{1,0:T(8,128)S(1)}, u32[]{:S(2)}, u32[]{:S(2)}) collective-permute-start(f32[256,128]{1,0:T(8,128)S(1)} %get-tuple-element.17), channel_id=1, source_target_pairs={{0,1},{1,2},{2,3},{3,4},{4,5},{5,6},{6,7},{8,9},{9,10},{10,11},{11... | collective-permute-start | bytes 393224 | tf_op jit(solution)/shard_map/ppermute | solution.py:18
  97.7 6.3 %collective-permute-start.1 = (f32[256,128]{1,0:T(8,128)S(1)}, f32[256,128]{1,0:T(8,128)S(1)}, u32[]{:S(2)}, u32[]{:S(2)}) collective-permute-start(f32[256,128]{1,0:T(8,128)S(1)} %get-tuple-element.18), channel_id=1, source_target_pairs={{1,0},{2,1},{3,2},{4,3},{5,4},{6,5},{7,6},{9,8},{10,9},{11,10},{12... | collective-permute-start | bytes 393224 | tf_op jit(solution)/shard_map/ppermute | solution.py:18
  168.0 4.3 %collective-permute-start.2 = (f32[256,128]{1,0:T(8,128)S(1)}, f32[256,128]{1,0:T(8,128)S(1)}, u32[]{:S(2)}, u32[]{:S(2)}) collective-permute-start(f32[256,128]{1,0:T(8,128)S(1)} %get-tuple-element.15), channel_id=1, source_target_pairs={{0,1},{1,2},{2,3},{3,4},{4,5},{5,6},{6,7},{8,9},{9,10},{10,11},{11... | collective-permute-start | bytes 393224 | tf_op jit(solution)/shard_map/ppermute | solution.py:18
  169.9 6.3 %collective-permute-start.3 = (f32[256,128]{1,0:T(8,128)S(1)}, f32[256,128]{1,0:T(8,128)S(1)}, u32[]{:S(2)}, u32[]{:S(2)}) collective-permute-start(f32[256,128]{1,0:T(8,128)S(1)} %get-tuple-element.16), channel_id=1, source_target_pairs={{1,0},{2,1},{3,2},{4,3},{5,4},{6,5},{7,6},{9,8},{10,9},{11,10},{12... | collective-permute-start | bytes 393224 | tf_op jit(solution)/shard_map/ppermute | solution.py:18
where the time goes:
time: 214 us; the launch traced here: 215 us
  Pallas kernels  128 us (60%)
  waiting for transfers between devices  31.6 us (15%)
  blocking collectives  28.4 us (13%)
  starting transfers between devices  14.5 us (7%)
  local copies, waits for them, and re-layouts  10.6 us (5%)
    pallas_call x1, Pallas kernels, body(): pl.pallas_call(second_kernel, out_shape=(z_shape, sent_shape, field_shape...  62.3 us
    pallas_call x1, Pallas kernels, body(): pl.pallas_call(first_kernel, out_shape=(z_shape, sent_shape), in_specs=[s...  58.9 us
    all_to_all x1, blocking collectives, body(): back = lax.all_to_all(done, 'mode', 0, 0, tiled=True)  28.4 us
    all_to_all x1, waiting for transfers between devices, body(): mine = lax.all_to_all(parts, 'mode', 0, 0, tiled=True)  23.4 us
    ppermute x4, starting transfers between devices, from_behind(): return lax.ppermute(block, axis, route)  10.8 us
    ppermute x4, waiting for transfers between devices, from_behind(): return lax.ppermute(block, axis, route)  8.22 us
    pallas_call x1, Pallas kernels, body(): pl.pallas_call(last_kernel, out_shape=field_shape, in_specs=[vmem] * 6, o...  6.73 us
    unnamed x6, local copies, waits for them, and re-layouts  4.57 us
  transfers between devices with their start and end apart: 5, of which 3 were waited for; matrix products, arithmetic and copies ran while one was open for 0% of the time, Pallas kernels for 0%

commit v1 on v0

--- a/solution.py
+++ b/solution.py
@@ -54,7 +54,7 @@
 def couple(x_ref, coef_ref, nu_modes_ref, h_ref):
     pieces, total = x_ref.shape[1], x_ref.shape[2] // 2
     rows = 2 * total
-    step = 64
+    step = 32
 
     @pl.loop(0, pieces)
     def _(nt):
@@ -77,69 +77,85 @@
                 h_ref[rows + base : rows + base + step, cols] = low
 
 
-def stiffness(h_ref, connect_ref, plane_ref, mode_ref, t_ref, p_ref, y_ref, z_ref):
+def one_hot(hit):
+    return jnp.where(hit, 1.0, 0.0).astype(bf16)
+
+
+def gather(h_ref, connect_ref, p_ref, t):
+    rows, nloc = h_ref.shape[0] // 2, h_ref.shape[1]
+
+    @pl.loop(0, 6)
+    def _(a):
+        ids = lax.broadcasted_iota(jnp.int32, (nloc, tile), 0)
+        table = one_hot(ids == connect_ref[pl.ds(a, 1), lane_slice(t, tile)])
+        both = jnp.dot(h_ref[...], table, preferred_element_type=f32)
+        p_ref[a] = both[:rows] + both[rows:]
+
+
+def elements(plane_ref, mode_ref, p_ref, y_ref, t):
+    rows = y_ref.shape[0] // 2
+    total = rows // 2
+    band = 16
+
+    @pl.loop(0, total // band)
+    def _(g):
+        at = pl.multiple_of(g * band, band)
+        m = lax.broadcasted_iota(jnp.int32, (band, lanes), 0) + at
+        mm = jnp.minimum(m, total - m).astype(f32)
+        weight = mm * mm
+        for piece in range(tile // lanes):
+            cols = pl.ds(pl.multiple_of(t * tile + piece * lanes, lanes), lanes)
+            near = slice(piece * lanes, (piece + 1) * lanes)
+            picked = [
+                [p_ref[a, pl.ds(part * total + at, band), near] for a in range(6)]
+                for part in range(2)
+            ]
+            y = [[jnp.zeros((band, lanes), f32)] * 6 for part in range(2)]
+            for b in range(6):
+                for a in range(b, 6):
+                    s = plane_ref[b, a : a + 1, cols] + weight * mode_ref[b, a : a + 1, cols]
+                    for part in range(2):
+                        y[part][b] = y[part][b] + s * picked[part][a]
+                        if a != b:
+                            y[part][a] = y[part][a] + s * picked[part][b]
+            for part in range(2):
+                for b in range(6):
+                    high, low = halves(y[part][b])
+                    here = slice(b * tile + piece * lanes, b * tile + (piece + 1) * lanes)
+                    base = part * total + at
+                    y_ref[pl.ds(pl.multiple_of(base, band), band), here] = high
+                    y_ref[pl.ds(pl.multiple_of(rows + base, band), band), here] = low
+
+
+def scatter(y_ref, columns_ref, z_ref, t):
     rows, nloc = z_ref.shape
-    total = rows // 2
+    chunk = 512
+
+    @pl.loop(0, nloc // chunk)
+    def _(n):
+        cols = lane_slice(n, chunk)
+        ids = lax.broadcasted_iota(jnp.int32, (tile, lanes), 1) + n * chunk
+        slots = []
+        for b in range(6):
+            nodes = columns_ref[b, lane_slice(t, tile), :]
+            pieces = [one_hot(ids + k * lanes == nodes) for k in range(chunk // lanes)]
+            slots.append(jnp.concatenate(pieces, axis=1))
+        table = jnp.concatenate(slots, axis=0)
+        both = jnp.dot(y_ref[...], table, preferred_element_type=f32)
+        z_ref[:, cols] += both[:rows] + both[rows:]
+
+
+def stiffness(h_ref, connect_ref, plane_ref, mode_ref, turned_ref, p_ref, y_ref, columns_ref, z_ref):
+    z_ref[...] = jnp.zeros_like(z_ref)
     elems = connect_ref.shape[1]
-    z_ref[...] = jnp.zeros_like(z_ref)
-    chunk = 256
-    band = 16
+    for b in range(6):
+        columns_ref[b] = jnp.broadcast_to(turned_ref[:, b : b + 1], (elems, lanes))
 
     @pl.loop(0, elems // tile)
     def _(t):
-        @pl.loop(0, nloc // chunk)
-        def _(n):
-            ids = lax.broadcasted_iota(jnp.int32, (chunk, tile), 0) + n * chunk
-            for a in range(6):
-                hit = ids == connect_ref[a : a + 1, lane_slice(t, tile)]
-                t_ref[lane_slice(n, chunk), a * tile : (a + 1) * tile] = jnp.where(
-                    hit, 1.0, 0.0
-                ).astype(bf16)
-
-        @pl.loop(0, 6)
-        def _(a):
-            both = jnp.dot(h_ref[...], t_ref[:, lane_slice(a, tile)], preferred_element_type=f32)
-            p_ref[a] = both[:rows] + both[rows:]
-
-        @pl.loop(0, total // band)
-        def _(g):
-            at = pl.multiple_of(g * band, band)
-            m = lax.broadcasted_iota(jnp.int32, (band, lanes), 0) + at
-            mm = jnp.minimum(m, total - m).astype(f32)
-            weight = mm * mm
-            for piece in range(tile // lanes):
-                cols = pl.ds(pl.multiple_of(t * tile + piece * lanes, lanes), lanes)
-                near = slice(piece * lanes, (piece + 1) * lanes)
-                picked = [
-                    [p_ref[a, pl.ds(part * total + at, band), near] for a in range(6)]
-                    for part in range(2)
-                ]
-                y = [[jnp.zeros((band, lanes), f32)] * 6 for part in range(2)]
-                for b in range(6):
-                    for a in range(b, 6):
-                        s = plane_ref[b, a : a + 1, cols] + weight * mode_ref[b, a : a + 1, cols]
-                        for part in range(2):
-                            y[part][b] = y[part][b] + s * picked[part][a]
-                            if a != b:
-                                y[part][a] = y[part][a] + s * picked[part][b]
-                for part in range(2):
-                    for b in range(6):
-                        high, low = halves(y[part][b])
-                        here = slice(b * tile + piece * lanes, b * tile + (piece + 1) * lanes)
-                        base = part * total + at
-                        y_ref[pl.ds(pl.multiple_of(base, band), band), here] = high
-                        y_ref[pl.ds(pl.multiple_of(rows + base, band), band), here] = low
-
-        @pl.loop(0, nloc // chunk)
-        def _(n):
-            cols = lane_slice(n, chunk)
-            both = lax.dot_general(
-                y_ref[...],
-                t_ref[cols, :],
-                (((1,), (1,)), ((), ())),
-                preferred_element_type=f32,
-            )
-            z_ref[:, cols] += both[:rows] + both[rows:]
+        gather(h_ref, connect_ref, p_ref, t)
+        elements(plane_ref, mode_ref, p_ref, y_ref, t)
+        scatter(y_ref, columns_ref, z_ref, t)
 
 
 def send_values(z_ref, h_ref, select_ref, sent_ref):
@@ -166,8 +182,8 @@
 
 
 def first_kernel(
-    nu_modes_ref, b_ref, coef_ref, connect_ref, plane_ref, mode_ref, shared_ref,
-    z_ref, sent_ref, x_ref, h_ref, t_ref, p_ref, y_ref, select_ref,
+    nu_modes_ref, b_ref, coef_ref, connect_ref, turned_ref, plane_ref, mode_ref, shared_ref,
+    z_ref, sent_ref, x_ref, h_ref, p_ref, y_ref, columns_ref, select_ref,
 ):
     sources, _, count, nloc = b_ref.shape
     fill_select(shared_ref, select_ref)
@@ -179,14 +195,14 @@
                 put_field(x_ref, part, nt, source * count, b_ref[source, part, :, lane_slice(nt, lanes)])
 
     couple(x_ref, coef_ref, nu_modes_ref, h_ref)
-    stiffness(h_ref, connect_ref, plane_ref, mode_ref, t_ref, p_ref, y_ref, z_ref)
+    stiffness(h_ref, connect_ref, plane_ref, mode_ref, turned_ref, p_ref, y_ref, columns_ref, z_ref)
     send_values(z_ref, h_ref, select_ref, sent_ref)
 
 
 def second_kernel(
-    nu_modes_ref, b_ref, coef_ref, connect_ref, plane_ref, mode_ref, shared_ref,
+    nu_modes_ref, b_ref, coef_ref, connect_ref, turned_ref, plane_ref, mode_ref, shared_ref,
     inv_ref, z1_ref, got_ref,
-    z_ref, sent_ref, mid_ref, x_ref, h_ref, t_ref, p_ref, y_ref, select_ref, split_ref,
+    z_ref, sent_ref, mid_ref, x_ref, h_ref, p_ref, y_ref, columns_ref, select_ref, split_ref,
 ):
     sources, _, count, nloc = b_ref.shape
     total = sources * count
@@ -210,7 +226,7 @@
                     put_field(x_ref, part, nt, source * count, value)
 
     couple(x_ref, coef_ref, nu_modes_ref, h_ref)
-    stiffness(h_ref, connect_ref, plane_ref, mode_ref, t_ref, p_ref, y_ref, z_ref)
+    stiffness(h_ref, connect_ref, plane_ref, mode_ref, turned_ref, p_ref, y_ref, columns_ref, z_ref)
     send_values(z_ref, h_ref, select_ref, sent_ref)
 
 
@@ -235,6 +251,96 @@
                 out_ref[source, part, :, cols] = 0.5 * b_ref[source, part, :, cols] + 0.5 * value
 
 
+def greet(devices):
+    me = lax.axis_index("mode")
+    barrier = pltpu.get_barrier_semaphore()
+    for k in range(1, devices):
+        pl.semaphore_signal(
+            barrier, inc=1, device_id={"mode": (me + k) % devices}, device_id_type=pl.DeviceIdType.MESH
+        )
+    pl.semaphore_wait(barrier, devices - 1)
+    return me
+
+
+def remote(source_ref, target_ref, send_sem, recv_sem, k, device):
+    return pltpu.make_async_remote_copy(
+        src_ref=source_ref, dst_ref=target_ref, send_sem=send_sem.at[k], recv_sem=recv_sem.at[k],
+        device_id={"mode": device}, device_id_type=pl.DeviceIdType.MESH,
+    )
+
+
+def spread_kernel(devices, comps, parts_ref, out_ref, send_sem, recv_sem, own_sem):
+    me = greet(devices)
+
+    def to(k):
+        other = (me + k) % devices
+        return other, other < comps
+
+    for k in range(1, devices):
+        other, wanted = to(k)
+
+        @pl.when(wanted)
+        def _():
+            remote(parts_ref.at[other], out_ref.at[me], send_sem, recv_sem, k, other).start()
+
+    @pl.when(me < comps)
+    def _():
+        own = pltpu.make_async_copy(parts_ref.at[me], out_ref.at[me], own_sem)
+        own.start()
+        own.wait()
+        for k in range(1, devices):
+            source = (me + devices - k) % devices
+            remote(out_ref.at[source], out_ref.at[source], send_sem, recv_sem, k, source).wait_recv()
+
+    for k in range(1, devices):
+        other, wanted = to(k)
+
+        @pl.when(wanted)
+        def _():
+            remote(parts_ref.at[other], out_ref.at[me], send_sem, recv_sem, k, other).wait_send()
+
+
+def collect_kernel(devices, comps, done_ref, out_ref, send_sem, recv_sem, own_sem):
+    me = greet(devices)
+
+    @pl.when(me < comps)
+    def _():
+        for k in range(1, devices):
+            other = (me + k) % devices
+            remote(done_ref.at[other], out_ref.at[me], send_sem, recv_sem, k, other).start()
+        own = pltpu.make_async_copy(done_ref.at[me], out_ref.at[me], own_sem)
+        own.start()
+        own.wait()
+
+    for k in range(1, devices):
+        source = (me + devices - k) % devices
+
+        @pl.when(source < comps)
+        def _():
+            remote(out_ref.at[source], out_ref.at[source], send_sem, recv_sem, k, source).wait_recv()
+
+    @pl.when(me < comps)
+    def _():
+        for k in range(1, devices):
+            other = (me + k) % devices
+            remote(done_ref.at[other], out_ref.at[me], send_sem, recv_sem, k, other).wait_send()
+
+
+def move(kernel, block, devices, comps, out_blocks, name):
+    where = pl.BlockSpec(memory_space=pl.ANY)
+    return pl.pallas_call(
+        functools.partial(kernel, devices, comps),
+        out_shape=jax.ShapeDtypeStruct((out_blocks,) + block.shape[1:], f32),
+        in_specs=[where], out_specs=where,
+        scratch_shapes=[
+            pltpu.SemaphoreType.DMA((devices,)),
+            pltpu.SemaphoreType.DMA((devices,)),
+            pltpu.SemaphoreType.DMA,
+        ],
+        compiler_params=pltpu.CompilerParams(collective_id=name, has_side_effects=True),
+    )(block)
+
+
 def exchange(sent):
     below = from_behind(sent[1], "mesh", 1)
     above = from_behind(sent[0], "mesh", -1)
@@ -247,8 +353,7 @@
     total = sources * count
     rows = 2 * total
     parts = jnp.transpose(b_field, (2, 1, 0, 3))
-    parts = jnp.pad(parts, ((0, sources - comps), (0, 0), (0, 0), (0, 0)))
-    mine = lax.all_to_all(parts, "mode", 0, 0, tiled=True)
+    mine = move(spread_kernel, parts, sources, comps, sources, 0)
     inv = inv_mass[None, :]
     shared = shared_nodes[0]
     vmem = pl.BlockSpec(memory_space=pltpu.VMEM)
@@ -257,30 +362,30 @@
     scratch = [
         pltpu.VMEM((2, nloc // lanes, 2 * total, lanes), f32),
         pltpu.VMEM((2 * rows, nloc), bf16),
-        pltpu.VMEM((nloc, 6 * tile), bf16),
         pltpu.VMEM((6, rows, tile), f32),
         pltpu.VMEM((2 * rows, 6 * tile), bf16),
+        pltpu.VMEM((6, connect.shape[1], lanes), jnp.int32),
         pltpu.VMEM((nloc, 2 * lanes), bf16),
     ]
     split = pltpu.VMEM((2 * rows, 2 * lanes), bf16)
     z_shape = jax.ShapeDtypeStruct((rows, nloc), f32)
     sent_shape = jax.ShapeDtypeStruct((2, rows, lanes), f32)
     field_shape = jax.ShapeDtypeStruct(mine.shape, f32)
-    fixed = (nu_coef, connect, stiff_plane, stiff_mode, shared)
+    fixed = (nu_coef, connect, connect.T, stiff_plane, stiff_mode, shared)
     z1, sent = pl.pallas_call(
-        first_kernel, out_shape=(z_shape, sent_shape), in_specs=[smem] + [vmem] * 6,
+        first_kernel, out_shape=(z_shape, sent_shape), in_specs=[smem] + [vmem] * 7,
         out_specs=(vmem, vmem), scratch_shapes=scratch, compiler_params=params,
     )(nu_modes, mine, *fixed)
     z2, sent2, mid = pl.pallas_call(
-        second_kernel, out_shape=(z_shape, sent_shape, field_shape), in_specs=[smem] + [vmem] * 9,
+        second_kernel, out_shape=(z_shape, sent_shape, field_shape), in_specs=[smem] + [vmem] * 10,
         out_specs=(vmem, vmem, vmem), scratch_shapes=scratch + [split], compiler_params=params,
     )(nu_modes, mine, *fixed, inv, z1, exchange(sent))
     done = pl.pallas_call(
         last_kernel, out_shape=field_shape, in_specs=[vmem] * 6, out_specs=vmem,
         scratch_shapes=[scratch[-1], split], compiler_params=params,
     )(mine, mid, shared, inv, z2, exchange(sent2))
-    back = lax.all_to_all(done, "mode", 0, 0, tiled=True)
-    return jnp.transpose(back[:comps], (2, 1, 0, 3))
+    back = move(collect_kernel, done, sources, comps, comps, 1)
+    return jnp.transpose(back, (2, 1, 0, 3))
 
 
 def solution(mesh):

time: 214 us -> 198 us (0.925)
  Pallas kernels: 128 us -> 165 us
  blocking collectives: 28.4 us -> 0 us
  waiting for transfers between devices: 31.6 us -> 8.22 us
  starting transfers between devices: 14.5 us -> 9.9 us
  local copies, waits for them, and re-layouts: 10.6 us -> 12.9 us
    pallas_call x0 -> x2, Pallas kernels: none -> 51.8 us  [move(): pl.pallas_call(functools.partial(kernel, devices, comps), out_shape=jax.S...]
    all_to_all x1 -> x0, blocking collectives: 28.4 us -> none  [body(): back = lax.all_to_all(done, 'mode', 0, 0, tiled=True)]
    all_to_all x1 -> x0, waiting for transfers between devices: 23.4 us -> none  [body(): mine = lax.all_to_all(parts, 'mode', 0, 0, tiled=True)]
    pallas_call x1, Pallas kernels: 62.3 us -> 54.9 us  [body(): pl.pallas_call(second_kernel, out_shape=(z_shape, sent_shape, field_shape...]
    pallas_call x1, Pallas kernels: 58.9 us -> 51.6 us  [body(): pl.pallas_call(first_kernel, out_shape=(z_shape, sent_shape), in_specs=[s...]
    all_to_all x1 -> x0, starting transfers between devices: 3.74 us -> none  [body(): mine = lax.all_to_all(parts, 'mode', 0, 0, tiled=True)]
    unnamed x6 -> x3, local copies, waits for them, and re-layouts: 4.57 us -> 7.2 us
  transfers between devices with their start and end apart: 5 -> 4, of which waited for: 3 -> 2; matrix products, arithmetic and copies ran while one was open for 0% -> 0% of each run, Pallas kernels for 0% -> 0%
where the time goes in v1:
time: 198 us
  Pallas kernels  165 us (83%)
  local copies, waits for them, and re-layouts  12.9 us (7%)
  starting transfers between devices  9.9 us (5%)
  waiting for transfers between devices  8.22 us (4%)
    pallas_call x1, Pallas kernels, body(): pl.pallas_call(second_kernel, out_shape=(z_shape, sent_shape, field_shape...  54.9 us
    pallas_call x2, Pallas kernels, move(): pl.pallas_call(functools.partial(kernel, devices, comps), out_shape=jax.S...  51.8 us
    pallas_call x1, Pallas kernels, body(): pl.pallas_call(first_kernel, out_shape=(z_shape, sent_shape), in_specs=[s...  51.6 us
    ppermute x4, starting transfers between devices, from_behind(): return lax.ppermute(block, axis, route)  9.9 us
    ppermute x4, waiting for transfers between devices, from_behind(): return lax.ppermute(block, axis, route)  8.22 us
    unnamed x3, local copies, waits for them, and re-layouts  7.2 us
    pallas_call x1, Pallas kernels, body(): pl.pallas_call(last_kernel, out_shape=field_shape, in_specs=[vmem] * 6, o...  6.75 us
  transfers between devices with their start and end apart: 4, of which 2 were waited for; matrix products, arithmetic and copies ran while one was open for 0% of the time, Pallas kernels for 0%

profile of v1, /device:TPU:9, one launch (start us, length us, event | category | flops | bytes accessed | tf_op | source)
XLA Modules:
  0.0 197.6 jit_solution(14565256107302010610)
XLA Ops:
  0.0 1.9 copy.12.coef_ref
  1.9 1.8 copy.10
  3.7 3.5 %copy.15 = f32[32,2,3,2048]{3,0,1,2:T(8,128)} copy(f32[32,2,3,2048]{3,1,2,0:T(2,128)} %param.8) | data formatting | bytes 3145728 | tf_op args[0]
  7.2 26.4 %shard_map.82.b_ref = f32[4,2,32,2048]{3,2,1,0:T(8,128)} custom-call(f32[3,2,32,2048]{3,2,1,0:T(8,128)} %bitcast.20), custom_call_target="tpu_custom_call" | custom-call | tf_op jit(solution)/shard_map/pallas_call | solution.py:331
  33.6 51.6 %shard_map.83 = (f32[256,2048]{1,0:T(8,128)}, f32[2,256,128]{2,1,0:T(8,128)}) custom-call(s32[17]{0:T(128)} %nu_modes_ref.3, f32[4,2,32,2048]{3,2,1,0:T(8,128)} %shard_map.82.b_ref, f32[2,17,2048]{2,1,0:T(8,128)} %copy.12.coef_ref, s32[6,1024]{1,0:T(8,128)} %connect_ref.3, s32[1024,6]{1,0:T(8,128)} %bitcast.21, f32[6,6,1024]{2,1,0:T(8,128)} %plane_ref.3, ...), custom_call_target="tpu_custom_call" | custom-call | tf_op jit(solution)/shard_map/pallas_call | solution.py:375
  85.3 1.0 slice_bitcast_fusion.3
  86.3 3.7 %collective-permute-start = (f32[256,128]{1,0:T(8,128)S(1)}, f32[256,128]{1,0:T(8,128)S(1)}, u32[]{:S(2)}, u32[]{:S(2)}) collective-permute-start(f32[256,128]{1,0:T(8,128)S(1)} %get-tuple-element.17), channel_id=1, source_target_pairs={{0,1},{1,2},{2,3},{3,4},{4,5},{5,6},{6,7},{8,9},{9,10},{10,11},{11... | collective-permute-start | bytes 393224 | tf_op jit(solution)/shard_map/ppermute | solution.py:18
  89.9 1.9 collective-permute-start.1
  91.8 0.0 collective-permute-done
  91.9 4.3 %collective-permute-done.1 = f32[256,128]{1,0:T(8,128)S(1)} collective-permute-done((f32[256,128]{1,0:T(8,128)S(1)}, f32[256,128]{1,0:T(8,128)S(1)}, u32[]{:S(2)}, u32[]{:S(2)}) %collective-permute-start.1) | collective-permute-done | bytes 131104 | tf_op jit(solution)/shard_map/ppermute | solution.py:18
  96.2 0.7 pad_maximum_fusion.got_ref
  96.9 54.9 %shard_map.84 = (f32[256,2048]{1,0:T(8,128)}, f32[2,256,128]{2,1,0:T(8,128)}, f32[4,2,32,2048]{3,2,1,0:T(8,128)}) custom-call(s32[17]{0:T(128)} %nu_modes_ref.3, f32[4,2,32,2048]{3,2,1,0:T(8,128)} %shard_map.82.b_ref, f32[2,17,2048]{2,1,0:T(8,128)} %copy.12.coef_ref, s32[6,1024]{1,0:T(8,128)} %connect_ref.3, s32[1024,6]{1,0:T(8,128)} %bitcast.22, ...), custom_call_target="tpu_custom_call" | custom-call | tf_op jit(solution)/shard_map/pallas_call | solution.py:379
  151.8 1.0 slice_bitcast_fusion.1
  152.8 1.9 collective-permute-start.2
  154.8 2.4 %collective-permute-start.3 = (f32[256,128]{1,0:T(8,128)S(1)}, f32[256,128]{1,0:T(8,128)S(1)}, u32[]{:S(2)}, u32[]{:S(2)}) collective-permute-start(f32[256,128]{1,0:T(8,128)S(1)} %get-tuple-element.16), channel_id=1, source_target_pairs={{1,0},{2,1},{3,2},{4,3},{5,4},{6,5},{7,6},{9,8},{10,9},{11,10},{12... | collective-permute-start | bytes 393224 | tf_op jit(solution)/shard_map/ppermute | solution.py:18
  157.2 0.0 collective-permute-done.2
  157.2 3.9 %collective-permute-done.3 = f32[256,128]{1,0:T(8,128)S(1)} collective-permute-done((f32[256,128]{1,0:T(8,128)S(1)}, f32[256,128]{1,0:T(8,128)S(1)}, u32[]{:S(2)}, u32[]{:S(2)}) %collective-permute-start.3) | collective-permute-done | bytes 131104 | tf_op jit(solution)/shard_map/ppermute | solution.py:18
  161.0 0.7 pad_maximum_fusion.1.got_ref
  161.8 6.7 %shard_map.85.done_ref = f32[4,2,32,2048]{3,2,1,0:T(8,128)} custom-call(f32[4,2,32,2048]{3,2,1,0:T(8,128)} %shard_map.82.b_ref, f32[4,2,32,2048]{3,2,1,0:T(8,128)} %get-tuple-element.12.mid_ref, s32[2,128]{1,0:T(2,128)} %bitcast.31, f32[1,2048]{1,0:T(1,128)} %bitcast.28, f32[256,2048]{1,0:T(8,128)} %get-tuple-element.13.z_ref, ...), custom_call_target="tpu_custom_call" | custom-call | tf_op jit(solution)/shard_map/pallas_call | solution.py:383
  168.5 25.3 %shard_map.86 = f32[3,2,32,2048]{3,2,1,0:T(8,128)} custom-call(f32[4,2,32,2048]{3,2,1,0:T(8,128)} %shard_map.85.done_ref), custom_call_target="tpu_custom_call" | custom-call | tf_op jit(solution)/shard_map/pallas_call | solution.py:331
  193.9 3.8 %copy.13 = f32[32,2,3,2048]{3,1,2,0:T(2,128)} copy(f32[32,2,3,2048]{3,0,1,2:T(8,128)} %bitcast.19) | data formatting | bytes 3145728 | tf_op jit(solution)/shard_map/transpose | solution.py:388
Async XLA Ops:
  86.3 5.6 %collective-permute-start = (f32[256,128]{1,0:T(8,128)S(1)}, f32[256,128]{1,0:T(8,128)S(1)}, u32[]{:S(2)}, u32[]{:S(2)}) collective-permute-start(f32[256,128]{1,0:T(8,128)S(1)} %get-tuple-element.17), channel_id=1, source_target_pairs={{0,1},{1,2},{2,3},{3,4},{4,5},{5,6},{6,7},{8,9},{9,10},{10,11},{11... | collective-permute-start | bytes 393224 | tf_op jit(solution)/shard_map/ppermute | solution.py:18
  89.9 6.3 %collective-permute-start.1 = (f32[256,128]{1,0:T(8,128)S(1)}, f32[256,128]{1,0:T(8,128)S(1)}, u32[]{:S(2)}, u32[]{:S(2)}) collective-permute-start(f32[256,128]{1,0:T(8,128)S(1)} %get-tuple-element.18), channel_id=1, source_target_pairs={{1,0},{2,1},{3,2},{4,3},{5,4},{6,5},{7,6},{9,8},{10,9},{11,10},{12... | collective-permute-start | bytes 393224 | tf_op jit(solution)/shard_map/ppermute | solution.py:18
  152.8 4.3 %collective-permute-start.2 = (f32[256,128]{1,0:T(8,128)S(1)}, f32[256,128]{1,0:T(8,128)S(1)}, u32[]{:S(2)}, u32[]{:S(2)}) collective-permute-start(f32[256,128]{1,0:T(8,128)S(1)} %get-tuple-element.15), channel_id=1, source_target_pairs={{0,1},{1,2},{2,3},{3,4},{4,5},{5,6},{6,7},{8,9},{9,10},{10,11},{11... | collective-permute-start | bytes 393224 | tf_op jit(solution)/shard_map/ppermute | solution.py:18
  154.8 6.3 %collective-permute-start.3 = (f32[256,128]{1,0:T(8,128)S(1)}, f32[256,128]{1,0:T(8,128)S(1)}, u32[]{:S(2)}, u32[]{:S(2)}) collective-permute-start(f32[256,128]{1,0:T(8,128)S(1)} %get-tuple-element.16), channel_id=1, source_target_pairs={{1,0},{2,1},{3,2},{4,3},{5,4},{6,5},{7,6},{9,8},{10,9},{11,10},{12... | collective-permute-start | bytes 393224 | tf_op jit(solution)/shard_map/ppermute | solution.py:18
